TPU v7x, 512 devices: a whole 4x4x16 slice. The times are simulated.
512 devices in a mesh: seq: 64 (over x, z), tp: 8 (over y, core).
Axes of the slice: x: 4, y: 4, z: 16, core: 2. Of those that a mesh axis runs over, the one named last changes fastest.
Arguments:
- queries: bfloat16 [8192, 4096], P('seq', 'tp'), may hold values from -6 to 6
- block_kv: bfloat16 [8192, 1792], P('seq'), may hold values from -6 to 6
- nb_states: bfloat16 [640, 128, 896], P('seq', 'tp'), may hold values from -6 to 6
- key_weight: bfloat16 [896, 4096], P('seq', 'tp'), may hold values from -1 to 1
- value_weight: bfloat16 [896, 4096], P('seq', 'tp'), may hold values from -0.1875 to 0.1875
- counts: int32 [128], P('seq'), may hold values from 2 to 8, as said below
- owner_slot: int32 [640], P('seq'), may hold values from 0 to 9, as said below
- out_grad: bfloat16 [8192, 4096], P('seq', 'tp'), may hold values from -6 to 6
Outputs:
- attended: bfloat16 [8192, 4096], P('seq', 'tp')
- query_grad: float32 [8192, 4096], P('seq', 'tp')
- key_grad: float32 [896, 4096], P('seq', 'tp')
- value_grad: float32 [896, 4096], P('seq', 'tp')
Inputs may be any that keep to these rules, and one draw needn't show every extreme that they name: `counts`: blocks 2k and 2k + 1 have 10 neighbours together, so each device's blocks have 10; a block with 8 occurs in every draw. `owner_slot`: each device's 10 entries (its neighbours in block order) are a permutation of 0 to 9; entry r stores the neighbour r // 2 devices further along seq, cyclically, in row r of that device's block of nb_states.
All inputs are finite; a program needn't handle non-finite values.
Results may differ from a plain program's by a relative error of at most 0.019.
The roundings to bfloat16 on the way count: a program that leaves them out, or rounds other values in their place, can miss the bound.
Values may be sent and summed in bfloat16 or wider, within the bound.
A program may use at most 64 MiB of HBM per device.

v0:
```python
import jax
import jax.numpy as jnp
from jax import lax
from jax.sharding import PartitionSpec as P

HS = 128
REACH = 5


def shifted(block, axis, distance):
    devices = range(lax.axis_size(axis))
    route = [((i - distance) % len(devices), i) for i in devices]
    return lax.ppermute(block, axis, route)


def build_table(counts, owner_slot, slot_count, block_count):
    block_ends = jnp.cumsum(counts)
    position = jnp.arange(slot_count, dtype=jnp.int32)
    block_of = jnp.sum((position[:, None] >= block_ends[None, :]).astype(jnp.int32), axis=1)
    slot_hot = (owner_slot[:, None] == position[None, :]).astype(jnp.float32)
    block_hot = (block_of[:, None] == jnp.arange(block_count, dtype=jnp.int32)[None, :]).astype(
        jnp.float32
    )
    return jnp.sum(slot_hot[:, :, None] * block_hot[:, None, :], axis=0)


def encode(states, keys_vals, head_size):
    slot_count, row_count, enc_width = states.shape
    head_count = enc_width // head_size
    block_len = keys_vals.shape[1]
    query_heads = states.reshape(slot_count, row_count, head_count, head_size)
    key_heads = keys_vals[:, :, :enc_width].reshape(slot_count, block_len, head_count, head_size)
    value_heads = keys_vals[:, :, enc_width:].reshape(slot_count, block_len, head_count, head_size)
    scores = jnp.einsum(
        "rqhd,rkhd->rhqk", query_heads, key_heads, preferred_element_type=jnp.float32
    ) * head_size ** (-0.5)
    weights = jax.nn.softmax(scores, axis=-1).astype(jnp.bfloat16)
    mixed_out = jnp.einsum(
        "rhqk,rkhd->rqhd", weights, value_heads, preferred_element_type=jnp.float32
    )
    return (
        states.astype(jnp.float32) + mixed_out.reshape(slot_count, row_count, enc_width)
    ).astype(jnp.bfloat16)


def attend(block_query, key_rows, value_rows, head_size):
    slot_count, block_len, query_width = block_query.shape
    head_count = query_width // head_size
    key_len = key_rows.shape[1]
    query_heads = block_query.reshape(slot_count, block_len, head_count, head_size)
    key_heads = key_rows.reshape(slot_count, key_len, head_count, head_size)
    value_heads = value_rows.reshape(slot_count, key_len, head_count, head_size)
    scores = jnp.einsum(
        "rqhd,rkhd->rhqk", query_heads, key_heads, preferred_element_type=jnp.float32
    ) * head_size ** (-0.5)
    peak_row = lax.stop_gradient(jnp.max(scores, axis=-1))
    weights = jnp.exp(scores - peak_row[..., None])
    row_total = jnp.sum(weights, axis=-1)
    rounded_w = weights.astype(jnp.bfloat16)
    partial_value = jnp.einsum(
        "rhqk,rkhd->rqhd", rounded_w, value_heads, preferred_element_type=jnp.float32
    )
    return (partial_value, peak_row, row_total, weights, rounded_w)


def attend_back(
    block_query, key_rows, value_rows, weights, rounded_w, push_grad, lift_grad, head_size
):
    slot_count, block_len, query_width = block_query.shape
    head_count = query_width // head_size
    key_len = key_rows.shape[1]
    scaling = head_size ** (-0.5)
    query_heads = block_query.reshape(slot_count, block_len, head_count, head_size)
    key_heads = key_rows.reshape(slot_count, key_len, head_count, head_size)
    value_heads = value_rows.reshape(slot_count, key_len, head_count, head_size)
    push_half = push_grad.astype(jnp.bfloat16)
    dprob = (
        jnp.einsum("rqhd,rkhd->rhqk", push_half, value_heads, preferred_element_type=jnp.float32)
        + lift_grad[..., None]
    )
    dscore = (weights * dprob).astype(jnp.bfloat16)
    dquery = (
        jnp.einsum("rhqk,rkhd->rqhd", dscore, key_heads, preferred_element_type=jnp.float32)
        * scaling
    )
    dkeys = (
        jnp.einsum("rhqk,rqhd->rkhd", dscore, query_heads, preferred_element_type=jnp.float32)
        * scaling
    ).astype(jnp.bfloat16)
    dvalues = jnp.einsum(
        "rhqk,rqhd->rkhd", rounded_w, push_half, preferred_element_type=jnp.float32
    ).astype(jnp.bfloat16)
    return (dquery, dkeys, dvalues)


def select_rows(slot_table, source):
    shape_tail = (1,) * (source.ndim - 1)
    return jnp.sum(slot_table.reshape(slot_table.shape + shape_tail) * source[None], axis=1)


def per_device(
    queries, block_kv, nb_states, key_weight, value_weight, counts, owner_slot, out_grad
):
    slot_count = owner_slot.shape[0]
    block_count = counts.shape[0]
    block_len = queries.shape[0] // block_count
    per_offset = slot_count // REACH
    enc_width = nb_states.shape[2]
    query_width = queries.shape[1]
    head_local = query_width // HS
    slot_table = build_table(counts, owner_slot, slot_count, block_count)
    picker = slot_table.astype(jnp.bfloat16)
    query_blocks = queries.reshape(block_count, block_len, query_width)
    kv_blocks = block_kv.reshape(block_count, block_len, block_kv.shape[1])
    query_sel = jnp.einsum(
        "rc,ctk->rtk", picker, query_blocks, preferred_element_type=jnp.float32
    ).astype(jnp.bfloat16)
    kv_sel = jnp.einsum(
        "rc,ctk->rtk", picker, kv_blocks, preferred_element_type=jnp.float32
    ).astype(jnp.bfloat16)

    def by_offset(values):
        return values.reshape((REACH, per_offset) + values.shape[1:])

    query_sel = by_offset(query_sel)
    kv_sel = by_offset(kv_sel)
    got_query = [query_sel[0]]
    got_kv = [kv_sel[0]]
    for offset in range(1, REACH):
        arrived = shifted((query_sel[offset], kv_sel[offset]), "seq", offset)
        got_query.append(arrived[0])
        got_kv.append(arrived[1])
    slot_query = jnp.concatenate(got_query, axis=0)
    slot_kv = jnp.concatenate(got_kv, axis=0)
    encoded_local = encode(nb_states, slot_kv, HS)
    encoded_full = lax.all_gather(encoded_local, "tp", axis=1, tiled=True)
    key_full, value_full = (
        lax.all_gather(key_weight, "seq", axis=0, tiled=True),
        lax.all_gather(value_weight, "seq", axis=0, tiled=True),
    )
    encoded_flat = encoded_full.reshape(-1, enc_width)
    key_rows = (
        jnp.dot(encoded_flat, key_full, preferred_element_type=jnp.float32)
        .astype(jnp.bfloat16)
        .reshape(slot_count, -1, query_width)
    )
    value_rows = (
        jnp.dot(encoded_flat, value_full, preferred_element_type=jnp.float32)
        .astype(jnp.bfloat16)
        .reshape(slot_count, -1, query_width)
    )
    partial_value, peak_row, row_total, weights, rounded_w = attend(
        slot_query, key_rows, value_rows, HS
    )
    part_out = by_offset(partial_value)
    part_peak = by_offset(peak_row)
    part_total = by_offset(row_total)
    returned = [(part_out[0], part_peak[0], part_total[0])]
    for offset in range(1, REACH):
        returned.append(
            shifted((part_out[offset], part_peak[offset], part_total[offset]), "seq", -offset)
        )
    src_partial = jnp.concatenate([item[0] for item in returned], axis=0)
    src_peak = jnp.concatenate([item[1] for item in returned], axis=0)
    src_total = jnp.concatenate([item[2] for item in returned], axis=0)
    member = jnp.transpose(slot_table, (1, 0)) > 0.5
    block_peak = jnp.max(jnp.where(member[:, :, None, None], src_peak[None], -jnp.inf), axis=1)
    slot_peak = select_rows(slot_table, block_peak)
    rescale = jnp.exp(src_peak - slot_peak)
    denominator = jnp.sum(slot_table[:, :, None, None] * (rescale * src_total)[:, None], axis=0)
    weight_term = jnp.transpose(rescale, (0, 2, 1))[..., None] * src_partial
    numerator = jnp.sum(slot_table[:, :, None, None, None] * weight_term[:, None], axis=0)
    mixed_out = numerator / jnp.transpose(denominator, (0, 2, 1))[..., None]
    attended = mixed_out.reshape(queries.shape).astype(jnp.bfloat16)
    grad_blocks = out_grad.reshape(block_count, block_len, head_local, HS).astype(jnp.float32)
    delta_row = jnp.sum(grad_blocks * mixed_out, axis=-1)
    factor = rescale / select_rows(slot_table, denominator)
    lift_grad = -(factor * select_rows(slot_table, jnp.transpose(delta_row, (0, 2, 1))))
    push_grad = jnp.transpose(factor, (0, 2, 1))[..., None] * select_rows(slot_table, grad_blocks)
    push_parts = by_offset(push_grad)
    lift_parts = by_offset(lift_grad)
    owner_push = [push_parts[0]]
    owner_lift = [lift_parts[0]]
    for offset in range(1, REACH):
        arrived = shifted((push_parts[offset], lift_parts[offset]), "seq", offset)
        owner_push.append(arrived[0])
        owner_lift.append(arrived[1])
    dquery, dkeys, dvalues = attend_back(
        slot_query,
        key_rows,
        value_rows,
        weights,
        rounded_w,
        jnp.concatenate(owner_push, axis=0),
        jnp.concatenate(owner_lift, axis=0),
        HS,
    )
    dquery_parts = by_offset(dquery)
    src_dquery = [dquery_parts[0]]
    for offset in range(1, REACH):
        src_dquery.append(
            shifted(dquery_parts[offset].astype(jnp.bfloat16), "seq", -offset).astype(jnp.float32)
        )
    slot_dquery = jnp.concatenate(src_dquery, axis=0)
    query_grad = jnp.sum(slot_table[:, :, None, None, None] * slot_dquery[:, None], axis=0).reshape(
        queries.shape
    )
    grads_flat = jnp.concatenate(
        [dkeys.reshape(-1, query_width), dvalues.reshape(-1, query_width)], axis=1
    )
    summed = lax.psum_scatter(
        lax.dot_general(
            encoded_flat, grads_flat, (((0,), (0,)), ((), ())), preferred_element_type=jnp.float32
        ),
        "seq",
        scatter_dimension=0,
        tiled=True,
    )
    return (attended, query_grad, summed[:, :query_width], summed[:, query_width:])


def solution(mesh):
    in_specs = (
        P("seq", "tp"),
        P("seq", None),
        P("seq", "tp", None),
        P("seq", "tp"),
        P("seq", "tp"),
        P("seq"),
        P("seq"),
        P("seq", "tp"),
    )
    out_specs = (P("seq", "tp"), P("seq", "tp"), P("seq", "tp"), P("seq", "tp"))
    return jax.shard_map(
        per_device, mesh=mesh, in_specs=in_specs, out_specs=out_specs, check_vma=False
    )
```

profile of v0, /device:TPU:1, one launch (start us, length us, event | category | flops | bytes accessed | tf_op | source)
XLA Modules:
  0.0 816.2 jit_solution(4272177228624127023)
XLA Ops:
  12.2 4.4 collective-permute-start.4
  16.5 4.9 collective-permute-start.5
  21.5 7.5 collective-permute-start.6
  28.9 7.0 collective-permute-start.7
  36.6 12.4 %collective-permute-done.5 = bf16[2,64,1792]{2,0,1:T(2,128)(2,1)S(1)} collective-permute-done((bf16[2,64,1792]{2,0,1:T(2,128)(2,1)S(1)}, bf16[2,64,1792]{2,0,1:T(2,128)(2,1)S(1)}, u32[]{:S(2)}, u32[]{:S(2)}) %collective-permute-start.5) | collective-permute-done | bytes 458784 | tf_op jit(solution)/shard_map/ppermute | solution.py:13
  49.0 40.2 %collective-permute-done.6 = bf16[2,64,1792]{2,0,1:T(2,128)(2,1)S(1)} collective-permute-done((bf16[2,64,1792]{2,0,1:T(2,128)(2,1)S(1)}, bf16[2,64,1792]{2,0,1:T(2,128)(2,1)S(1)}, u32[]{:S(2)}, u32[]{:S(2)}) %collective-permute-start.6) | collective-permute-done | bytes 458784 | tf_op jit(solution)/shard_map/ppermute | solution.py:13
  89.2 9.1 %collective-permute-done.7 = bf16[2,64,1792]{2,0,1:T(2,128)(2,1)S(1)} collective-permute-done((bf16[2,64,1792]{2,0,1:T(2,128)(2,1)S(1)}, bf16[2,64,1792]{2,0,1:T(2,128)(2,1)S(1)}, u32[]{:S(2)}, u32[]{:S(2)}) %collective-permute-start.7) | collective-permute-done | bytes 458784 | tf_op jit(solution)/shard_map/ppermute | solution.py:13
  98.3 11.8 %concatenate.57 = bf16[10,64,1792]{2,0,1:T(8,128)(2,1)} concatenate(bf16[2,64,1792]{2,0,1:T(2,128)(2,1)S(1)} %get-tuple-element.18, bf16[2,64,1792]{2,0,1:T(2,128)(2,1)S(1)} %collective-permute-done.4, bf16[2,64,1792]{2,0,1:T(2,128)(2,1)S(1)} %collective-permute-done.5, bf16[2,64,1792]{2,0,1:T(2,128)(2,1)S(1)} %collective-permute-done.6, ...), dimensions={0} | concatenate | bytes 4587520 | tf_op jit(solution)/shard_map/concatenate | solution.py:134
  124.8 12.7 %collective-permute-start = (bf16[2,64,512]{2,0,1:T(2,128)(2,1)S(1)}, bf16[2,64,512]{2,0,1:T(2,128)(2,1)S(1)}, u32[]{:S(2)}, u32[]{:S(2)}) collective-permute-start(bf16[2,64,512]{2,0,1:T(2,128)(2,1)S(1)} %get-tuple-element.27), channel_id=1, source_target_pairs={{504,0},{0,8},{8,16},{16,24},{24,32},{32,40},{40,48},{48,56},{56,6... | collective-permute-start | bytes 393224 | tf_op jit(solution)/shard_map/ppermute | solution.py:13
  137.5 21.2 %collective-permute-start.1 = (bf16[2,64,512]{2,0,1:T(2,128)(2,1)S(1)}, bf16[2,64,512]{2,0,1:T(2,128)(2,1)S(1)}, u32[]{:S(2)}, u32[]{:S(2)}) collective-permute-start(bf16[2,64,512]{2,0,1:T(2,128)(2,1)S(1)} %get-tuple-element.26), channel_id=1, source_target_pairs={{496,0},{504,8},{0,16},{8,24},{16,32},{24,40},{32,48},{40,56},{48,... | collective-permute-start | bytes 393224 | tf_op jit(solution)/shard_map/ppermute | solution.py:13
  162.6 89.8 %all-gather = bf16[64,14,512]{2,1,0:T(8,128)(2,1)S(1)} all-gather(bf16[1,14,512]{2,1,0:T(8,128)(2,1)S(1)} %bitcast.111), channel_id=1, replica_groups=mesh['seq'=64,'tp'=8] {'seq'}, dimensions={0}, use_global_device_ids=true | all-gather | bytes 931840 | tf_op jit(solution)/shard_map/all_gather | solution.py:138
  253.8 75.0 %all-gather.1 = bf16[64,14,512]{2,1,0:T(8,128)(2,1)S(1)} all-gather(bf16[1,14,512]{2,1,0:T(8,128)(2,1)S(1)} %bitcast.112), channel_id=1, replica_groups=mesh['seq'=64,'tp'=8] {'seq'}, dimensions={0}, use_global_device_ids=true | all-gather | bytes 931840 | tf_op jit(solution)/shard_map/all_gather | solution.py:139
  336.7 4.4 collective-permute-start.8
  344.4 3.7 collective-permute-start.10
  348.2 4.3 collective-permute-start.11
  367.1 3.8 collective-permute-start.18
  371.0 5.6 collective-permute-start.19
  382.5 4.0 collective-permute-start.14
  386.6 5.1 collective-permute-start.15
  391.9 5.8 collective-permute-done.14
  397.8 10.4 %collective-permute-done.15 = f32[2,64,4,128]{3,1,2,0:T(8,128)S(1)} collective-permute-done((f32[2,64,4,128]{3,1,2,0:T(8,128)S(1)}, f32[2,64,4,128]{3,1,2,0:T(8,128)S(1)}, u32[]{:S(2)}, u32[]{:S(2)}) %collective-permute-start.15) | collective-permute-done | bytes 262176 | tf_op jit(solution)/shard_map/ppermute | solution.py:13
  411.8 6.6 collective-permute-start.24
  420.3 4.1 collective-permute-start.26
  424.5 4.9 collective-permute-start.27
  433.4 5.7 collective-permute-start.21
  439.1 4.6 collective-permute-start.22
  447.0 5.2 collective-permute-done.22
  452.3 7.1 collective-permute-done.23
  472.6 4.5 fusion.1
  485.0 4.7 collective-permute-start.30
  492.6 11.0 %collective-permute-done.31 = bf16[2,64,4,128]{3,1,2,0:T(8,128)(2,1)S(1)} collective-permute-done((bf16[2,64,4,128]{3,1,2,0:T(8,128)(2,1)S(1)}, bf16[2,64,4,128]{3,1,2,0:T(8,128)(2,1)S(1)}, u32[]{:S(2)}, u32[]{:S(2)}) %collective-permute-start.31) | collective-permute-done | bytes 131104 | tf_op jit(solution)/shard_map/ppermute | solution.py:13
  504.8 303.0 %all-reduce.3.cloned.1.call-done = f32[896,1024]{1,0:T(8,128)} async-done(((f32[896,1024]{1,0:T(8,128)}), f32[896,1024]{1,0:T(8,128)}) %all-reduce.3.cloned.1.call-update) | async-done | bytes 3670032
  (180 shorter events, 96.0 us)
Async XLA Ops:
  7.2 324.3 %all-gather.4.cloned.1.call-start = ((), (), s32[]{:S(2)}) async-start(), calls=%async_computation | async-start | bytes 2580480 | tf_op jit(solution)/shard_map/all_gather | solution.py:136
  12.2 24.4 %collective-permute-start.4 = (bf16[2,64,1792]{2,0,1:T(2,128)(2,1)S(1)}, bf16[2,64,1792]{2,0,1:T(2,128)(2,1)S(1)}, u32[]{:S(2)}, u32[]{:S(2)}) collective-permute-start(bf16[2,64,1792]{2,0,1:T(2,128)(2,1)S(1)} %get-tuple-element.17), channel_id=1, source_target_pairs={{504,0},{0,8},{8,16},{16,24},{24,32},{32,40},{40,48},{48,56},{56,6... | collective-permute-start | bytes 1376264 | tf_op jit(solution)/shard_map/ppermute | solution.py:13
  16.5 32.4 %collective-permute-start.5 = (bf16[2,64,1792]{2,0,1:T(2,128)(2,1)S(1)}, bf16[2,64,1792]{2,0,1:T(2,128)(2,1)S(1)}, u32[]{:S(2)}, u32[]{:S(2)}) collective-permute-start(bf16[2,64,1792]{2,0,1:T(2,128)(2,1)S(1)} %get-tuple-element.16), channel_id=1, source_target_pairs={{496,0},{504,8},{0,16},{8,24},{16,32},{24,40},{32,48},{40,56},{48,... | collective-permute-start | bytes 1376264 | tf_op jit(solution)/shard_map/ppermute | solution.py:13
  21.5 67.7 %collective-permute-start.6 = (bf16[2,64,1792]{2,0,1:T(2,128)(2,1)S(1)}, bf16[2,64,1792]{2,0,1:T(2,128)(2,1)S(1)}, u32[]{:S(2)}, u32[]{:S(2)}) collective-permute-start(bf16[2,64,1792]{2,0,1:T(2,128)(2,1)S(1)} %get-tuple-element.15), channel_id=1, source_target_pairs={{488,0},{496,8},{504,16},{0,24},{8,32},{16,40},{24,48},{32,56},{40... | collective-permute-start | bytes 1376264 | tf_op jit(solution)/shard_map/ppermute | solution.py:13
  28.9 69.4 %collective-permute-start.7 = (bf16[2,64,1792]{2,0,1:T(2,128)(2,1)S(1)}, bf16[2,64,1792]{2,0,1:T(2,128)(2,1)S(1)}, u32[]{:S(2)}, u32[]{:S(2)}) collective-permute-start(bf16[2,64,1792]{2,0,1:T(2,128)(2,1)S(1)} %get-tuple-element.14), channel_id=1, source_target_pairs={{480,0},{488,8},{496,16},{504,24},{0,32},{8,40},{16,48},{24,56},{3... | collective-permute-start | bytes 1376264 | tf_op jit(solution)/shard_map/ppermute | solution.py:13
  123.8 684.0 %all-reduce.3.cloned.1.call-start = ((), (), s32[]{:S(2)}) async-start(), calls=%async_computation.1 | async-start | bytes 7340032
  124.8 206.0 %collective-permute-start = (bf16[2,64,512]{2,0,1:T(2,128)(2,1)S(1)}, bf16[2,64,512]{2,0,1:T(2,128)(2,1)S(1)}, u32[]{:S(2)}, u32[]{:S(2)}) collective-permute-start(bf16[2,64,512]{2,0,1:T(2,128)(2,1)S(1)} %get-tuple-element.27), channel_id=1, source_target_pairs={{504,0},{0,8},{8,16},{16,24},{24,32},{32,40},{40,48},{48,56},{56,6... | collective-permute-start | bytes 393224 | tf_op jit(solution)/shard_map/ppermute | solution.py:13
  137.5 193.4 %collective-permute-start.1 = (bf16[2,64,512]{2,0,1:T(2,128)(2,1)S(1)}, bf16[2,64,512]{2,0,1:T(2,128)(2,1)S(1)}, u32[]{:S(2)}, u32[]{:S(2)}) collective-permute-start(bf16[2,64,512]{2,0,1:T(2,128)(2,1)S(1)} %get-tuple-element.26), channel_id=1, source_target_pairs={{496,0},{504,8},{0,16},{8,24},{16,32},{24,40},{32,48},{40,56},{48,... | collective-permute-start | bytes 393224 | tf_op jit(solution)/shard_map/ppermute | solution.py:13
  158.7 172.4 %collective-permute-start.2 = (bf16[2,64,512]{2,0,1:T(2,128)(2,1)S(1)}, bf16[2,64,512]{2,0,1:T(2,128)(2,1)S(1)}, u32[]{:S(2)}, u32[]{:S(2)}) collective-permute-start(bf16[2,64,512]{2,0,1:T(2,128)(2,1)S(1)} %get-tuple-element.25), channel_id=1, source_target_pairs={{488,0},{496,8},{504,16},{0,24},{8,32},{16,40},{24,48},{32,56},{40... | collective-permute-start | bytes 393224 | tf_op jit(solution)/shard_map/ppermute | solution.py:13
  160.6 170.6 %collective-permute-start.3 = (bf16[2,64,512]{2,0,1:T(2,128)(2,1)S(1)}, bf16[2,64,512]{2,0,1:T(2,128)(2,1)S(1)}, u32[]{:S(2)}, u32[]{:S(2)}) collective-permute-start(bf16[2,64,512]{2,0,1:T(2,128)(2,1)S(1)} %get-tuple-element.24), channel_id=1, source_target_pairs={{480,0},{488,8},{496,16},{504,24},{0,32},{8,40},{16,48},{24,56},{3... | collective-permute-start | bytes 393224 | tf_op jit(solution)/shard_map/ppermute | solution.py:13
  336.7 26.7 %collective-permute-start.8 = (f32[2,4,64]{2,1,0:T(4,128)S(1)}, f32[2,4,64]{2,1,0:T(4,128)S(1)}, u32[]{:S(2)}, u32[]{:S(2)}) collective-permute-start(f32[2,4,64]{2,1,0:T(4,128)S(1)} %get-tuple-element.55), channel_id=1, source_target_pairs={{8,0},{16,8},{24,16},{32,24},{40,32},{48,40},{56,48},{64,56},{72,6... | collective-permute-start | bytes 6152 | tf_op jit(solution)/shard_map/ppermute | solution.py:13
  341.1 26.0 %collective-permute-start.9 = (f32[2,4,64]{2,1,0:T(4,128)S(1)}, f32[2,4,64]{2,1,0:T(4,128)S(1)}, u32[]{:S(2)}, u32[]{:S(2)}) collective-permute-start(f32[2,4,64]{2,1,0:T(4,128)S(1)} %get-tuple-element.54), channel_id=1, source_target_pairs={{16,0},{24,8},{32,16},{40,24},{48,32},{56,40},{64,48},{72,56},{80,... | collective-permute-start | bytes 6152 | tf_op jit(solution)/shard_map/ppermute | solution.py:13
  344.4 26.5 %collective-permute-start.10 = (f32[2,4,64]{2,1,0:T(4,128)S(1)}, f32[2,4,64]{2,1,0:T(4,128)S(1)}, u32[]{:S(2)}, u32[]{:S(2)}) collective-permute-start(f32[2,4,64]{2,1,0:T(4,128)S(1)} %get-tuple-element.53), channel_id=1, source_target_pairs={{24,0},{32,8},{40,16},{48,24},{56,32},{64,40},{72,48},{80,56},{88,... | collective-permute-start | bytes 6152 | tf_op jit(solution)/shard_map/ppermute | solution.py:13
  348.2 28.4 %collective-permute-start.11 = (f32[2,4,64]{2,1,0:T(4,128)S(1)}, f32[2,4,64]{2,1,0:T(4,128)S(1)}, u32[]{:S(2)}, u32[]{:S(2)}) collective-permute-start(f32[2,4,64]{2,1,0:T(4,128)S(1)} %get-tuple-element.52), channel_id=1, source_target_pairs={{32,0},{40,8},{48,16},{56,24},{64,32},{72,40},{80,48},{88,56},{96,... | collective-permute-start | bytes 6152 | tf_op jit(solution)/shard_map/ppermute | solution.py:13
  353.3 26.7 %collective-permute-start.16 = (f32[2,4,64]{2,1,0:T(4,128)S(1)}, f32[2,4,64]{2,1,0:T(4,128)S(1)}, u32[]{:S(2)}, u32[]{:S(2)}) collective-permute-start(f32[2,4,64]{2,1,0:T(4,128)S(1)} %get-tuple-element.50), channel_id=1, source_target_pairs={{8,0},{16,8},{24,16},{32,24},{40,32},{48,40},{56,48},{64,56},{72,6... | collective-permute-start | bytes 6152 | tf_op jit(solution)/shard_map/ppermute | solution.py:13
  363.4 19.1 %collective-permute-start.17 = (f32[2,4,64]{2,1,0:T(4,128)S(1)}, f32[2,4,64]{2,1,0:T(4,128)S(1)}, u32[]{:S(2)}, u32[]{:S(2)}) collective-permute-start(f32[2,4,64]{2,1,0:T(4,128)S(1)} %get-tuple-element.49), channel_id=1, source_target_pairs={{16,0},{24,8},{32,16},{40,24},{48,32},{56,40},{64,48},{72,56},{80,... | collective-permute-start | bytes 6152 | tf_op jit(solution)/shard_map/ppermute | solution.py:13
  367.1 19.4 %collective-permute-start.18 = (f32[2,4,64]{2,1,0:T(4,128)S(1)}, f32[2,4,64]{2,1,0:T(4,128)S(1)}, u32[]{:S(2)}, u32[]{:S(2)}) collective-permute-start(f32[2,4,64]{2,1,0:T(4,128)S(1)} %get-tuple-element.48), channel_id=1, source_target_pairs={{24,0},{32,8},{40,16},{48,24},{56,32},{64,40},{72,48},{80,56},{88,... | collective-permute-start | bytes 6152 | tf_op jit(solution)/shard_map/ppermute | solution.py:13
  371.0 20.7 %collective-permute-start.19 = (f32[2,4,64]{2,1,0:T(4,128)S(1)}, f32[2,4,64]{2,1,0:T(4,128)S(1)}, u32[]{:S(2)}, u32[]{:S(2)}) collective-permute-start(f32[2,4,64]{2,1,0:T(4,128)S(1)} %get-tuple-element.47), channel_id=1, source_target_pairs={{32,0},{40,8},{48,16},{56,24},{64,32},{72,40},{80,48},{88,56},{96,... | collective-permute-start | bytes 6152 | tf_op jit(solution)/shard_map/ppermute | solution.py:13
  376.6 15.2 %collective-permute-start.12 = (f32[2,64,4,128]{3,1,2,0:T(8,128)S(1)}, f32[2,64,4,128]{3,1,2,0:T(8,128)S(1)}, u32[]{:S(2)}, u32[]{:S(2)}) collective-permute-start(f32[2,64,4,128]{3,1,2,0:T(8,128)S(1)} %get-tuple-element.22), channel_id=1, source_target_pairs={{8,0},{16,8},{24,16},{32,24},{40,32},{48,40},{56,48},{64,56},{72,6... | collective-permute-start | bytes 786440 | tf_op jit(solution)/shard_map/ppermute | solution.py:13
  380.0 11.9 %collective-permute-start.13 = (f32[2,64,4,128]{3,1,2,0:T(8,128)S(1)}, f32[2,64,4,128]{3,1,2,0:T(8,128)S(1)}, u32[]{:S(2)}, u32[]{:S(2)}) collective-permute-start(f32[2,64,4,128]{3,1,2,0:T(8,128)S(1)} %get-tuple-element.21), channel_id=1, source_target_pairs={{16,0},{24,8},{32,16},{40,24},{48,32},{56,40},{64,48},{72,56},{80,... | collective-permute-start | bytes 786440 | tf_op jit(solution)/shard_map/ppermute | solution.py:13
  382.5 15.2 %collective-permute-start.14 = (f32[2,64,4,128]{3,1,2,0:T(8,128)S(1)}, f32[2,64,4,128]{3,1,2,0:T(8,128)S(1)}, u32[]{:S(2)}, u32[]{:S(2)}) collective-permute-start(f32[2,64,4,128]{3,1,2,0:T(8,128)S(1)} %get-tuple-element.20), channel_id=1, source_target_pairs={{24,0},{32,8},{40,16},{48,24},{56,32},{64,40},{72,48},{80,56},{88,... | collective-permute-start | bytes 786440 | tf_op jit(solution)/shard_map/ppermute | solution.py:13
  386.6 21.6 %collective-permute-start.15 = (f32[2,64,4,128]{3,1,2,0:T(8,128)S(1)}, f32[2,64,4,128]{3,1,2,0:T(8,128)S(1)}, u32[]{:S(2)}, u32[]{:S(2)}) collective-permute-start(f32[2,64,4,128]{3,1,2,0:T(8,128)S(1)} %get-tuple-element.19), channel_id=1, source_target_pairs={{32,0},{40,8},{48,16},{56,24},{64,32},{72,40},{80,48},{88,56},{96,... | collective-permute-start | bytes 786440 | tf_op jit(solution)/shard_map/ppermute | solution.py:13
  411.8 21.5 %collective-permute-start.24 = (f32[2,4,64]{2,1,0:T(4,128)S(1)}, f32[2,4,64]{2,1,0:T(4,128)S(1)}, u32[]{:S(2)}, u32[]{:S(2)}) collective-permute-start(f32[2,4,64]{2,1,0:T(4,128)S(1)} %get-tuple-element.45), channel_id=1, source_target_pairs={{504,0},{0,8},{8,16},{16,24},{24,32},{32,40},{40,48},{48,56},{56,6... | collective-permute-start | bytes 6152 | tf_op jit(solution)/shard_map/ppermute | solution.py:13
  418.4 20.6 %collective-permute-start.25 = (f32[2,4,64]{2,1,0:T(4,128)S(1)}, f32[2,4,64]{2,1,0:T(4,128)S(1)}, u32[]{:S(2)}, u32[]{:S(2)}) collective-permute-start(f32[2,4,64]{2,1,0:T(4,128)S(1)} %get-tuple-element.44), channel_id=1, source_target_pairs={{496,0},{504,8},{0,16},{8,24},{16,32},{24,40},{32,48},{40,56},{48,... | collective-permute-start | bytes 6152 | tf_op jit(solution)/shard_map/ppermute | solution.py:13
  420.3 23.3 %collective-permute-start.26 = (f32[2,4,64]{2,1,0:T(4,128)S(1)}, f32[2,4,64]{2,1,0:T(4,128)S(1)}, u32[]{:S(2)}, u32[]{:S(2)}) collective-permute-start(f32[2,4,64]{2,1,0:T(4,128)S(1)} %get-tuple-element.43), channel_id=1, source_target_pairs={{488,0},{496,8},{504,16},{0,24},{8,32},{16,40},{24,48},{32,56},{40... | collective-permute-start | bytes 6152 | tf_op jit(solution)/shard_map/ppermute | solution.py:13
  424.5 22.4 %collective-permute-start.27 = (f32[2,4,64]{2,1,0:T(4,128)S(1)}, f32[2,4,64]{2,1,0:T(4,128)S(1)}, u32[]{:S(2)}, u32[]{:S(2)}) collective-permute-start(f32[2,4,64]{2,1,0:T(4,128)S(1)} %get-tuple-element.42), channel_id=1, source_target_pairs={{480,0},{488,8},{496,16},{504,24},{0,32},{8,40},{16,48},{24,56},{3... | collective-permute-start | bytes 6152 | tf_op jit(solution)/shard_map/ppermute | solution.py:13
  431.2 15.8 %collective-permute-start.20 = (bf16[2,64,4,128]{3,1,2,0:T(8,128)(2,1)S(1)}, bf16[2,64,4,128]{3,1,2,0:T(8,128)(2,1)S(1)}, u32[]{:S(2)}, u32[]{:S(2)}) collective-permute-start(bf16[2,64,4,128]{3,1,2,0:T(8,128)(2,1)S(1)} %get-tuple-element.36), channel_id=1, source_target_pairs={{504,0},{0,8},{8,16},{16,24},{24,32},{32,40},{40,48},{48,56},{56,6... | collective-permute-start | bytes 393224 | tf_op jit(solution)/shard_map/ppermute | solution.py:13
  433.4 13.6 %collective-permute-start.21 = (bf16[2,64,4,128]{3,1,2,0:T(8,128)(2,1)S(1)}, bf16[2,64,4,128]{3,1,2,0:T(8,128)(2,1)S(1)}, u32[]{:S(2)}, u32[]{:S(2)}) collective-permute-start(bf16[2,64,4,128]{3,1,2,0:T(8,128)(2,1)S(1)} %get-tuple-element.35), channel_id=1, source_target_pairs={{496,0},{504,8},{0,16},{8,24},{16,32},{24,40},{32,48},{40,56},{48,... | collective-permute-start | bytes 393224 | tf_op jit(solution)/shard_map/ppermute | solution.py:13
  439.1 13.2 %collective-permute-start.22 = (bf16[2,64,4,128]{3,1,2,0:T(8,128)(2,1)S(1)}, bf16[2,64,4,128]{3,1,2,0:T(8,128)(2,1)S(1)}, u32[]{:S(2)}, u32[]{:S(2)}) collective-permute-start(bf16[2,64,4,128]{3,1,2,0:T(8,128)(2,1)S(1)} %get-tuple-element.34), channel_id=1, source_target_pairs={{488,0},{496,8},{504,16},{0,24},{8,32},{16,40},{24,48},{32,56},{40... | collective-permute-start | bytes 393224 | tf_op jit(solution)/shard_map/ppermute | solution.py:13
  443.7 15.7 %collective-permute-start.23 = (bf16[2,64,4,128]{3,1,2,0:T(8,128)(2,1)S(1)}, bf16[2,64,4,128]{3,1,2,0:T(8,128)(2,1)S(1)}, u32[]{:S(2)}, u32[]{:S(2)}) collective-permute-start(bf16[2,64,4,128]{3,1,2,0:T(8,128)(2,1)S(1)} %get-tuple-element.33), channel_id=1, source_target_pairs={{480,0},{488,8},{496,16},{504,24},{0,32},{8,40},{16,48},{24,56},{3... | collective-permute-start | bytes 393224 | tf_op jit(solution)/shard_map/ppermute | solution.py:13
  480.4 11.8 %collective-permute-start.28 = (bf16[2,64,4,128]{3,1,2,0:T(8,128)(2,1)S(1)}, bf16[2,64,4,128]{3,1,2,0:T(8,128)(2,1)S(1)}, u32[]{:S(2)}, u32[]{:S(2)}) collective-permute-start(bf16[2,64,4,128]{3,1,2,0:T(8,128)(2,1)S(1)} %get-tuple-element.32), channel_id=1, source_target_pairs={{8,0},{16,8},{24,16},{32,24},{40,32},{48,40},{56,48},{64,56},{72,6... | collective-permute-start | bytes 393224 | tf_op jit(solution)/shard_map/ppermute | solution.py:13
  489.8 13.8 %collective-permute-start.31 = (bf16[2,64,4,128]{3,1,2,0:T(8,128)(2,1)S(1)}, bf16[2,64,4,128]{3,1,2,0:T(8,128)(2,1)S(1)}, u32[]{:S(2)}, u32[]{:S(2)}) collective-permute-start(bf16[2,64,4,128]{3,1,2,0:T(8,128)(2,1)S(1)} %get-tuple-element.29), channel_id=1, source_target_pairs={{32,0},{40,8},{48,16},{56,24},{64,32},{72,40},{80,48},{88,56},{96,... | collective-permute-start | bytes 393224 | tf_op jit(solution)/shard_map/ppermute | solution.py:13
  (23 other events, 523.5 us)
Sparse Core Ops, SparseCore 0:
  123.9 56.6 all-gather.3
  477.2 330.5 all-reduce.2
where the time goes:
time: 826 us; the launch traced here: 816 us
  waiting for transfers between devices  405 us (49%)
  blocking collectives  165 us (20%)
  starting transfers between devices  152 us (18%)
  local copies, waits for them, and re-layouts  44.7 us (5%)
  matrix products  24.5 us (3%)
  between operations  15.7 us (2%)
  other arithmetic  9.05 us (1%)
    unnamed x3, waiting for transfers between devices  303 us
    ppermute x32, starting transfers between devices, shifted(): return lax.ppermute(block, axis, route)  152 us
    ppermute x32, waiting for transfers between devices, shifted(): return lax.ppermute(block, axis, route)  102 us
    all_gather x1, blocking collectives, per_device(): lax.all_gather(key_weight, 'seq', axis=0, tiled=True)  89.8 us
    all_gather x1, blocking collectives, per_device(): lax.all_gather(value_weight, 'seq', axis=0, tiled=True)  75 us
  transfers between devices with their start and end apart: 34, of which 11 were waited for; matrix products, arithmetic and copies ran while one was open for 2% of the time, Pallas kernels for 0%

commit v1 on v0

v1 whole, which is shorter than its diff:
```python
import functools

import jax
import jax.numpy as jnp
import numpy as np
from jax import lax
from jax.experimental import pallas as pl
from jax.experimental.pallas import tpu as pltpu
from jax.sharding import PartitionSpec as P

HS = 128
REACH = 5
PAD = 16
QUAD = 4
MESH = pl.DeviceIdType.MESH
F32 = jnp.float32
BF16 = jnp.bfloat16


def dot(a, b, dims=((1,), (0,))):
    return lax.dot_general(a, b, (dims, ((), ())), preferred_element_type=F32)


class Sems:
    def __init__(self, send, recv):
        self.send, self.recv, self.used = send, recv, 0
        self.copies = []

    def copy(self, src, dst, device):
        i = self.used
        self.used += 1
        c = pltpu.make_async_remote_copy(
            src_ref=src,
            dst_ref=dst,
            send_sem=self.send.at[i],
            recv_sem=self.recv.at[i],
            device_id=device,
            device_id_type=MESH,
        )
        c.start()
        self.copies.append(c)
        return c

    def finish(self):
        for c in self.copies:
            c.wait_send()


def landed(copies):
    for c in copies:
        c.wait_recv()


def kernel(
    sizes,
    q_ref,
    kv_ref,
    nb_ref,
    wk_ref,
    wv_ref,
    counts_ref,
    owner_ref,
    g_ref,
    att_ref,
    dq_ref,
    gk_ref,
    gv_ref,
    nbf,
    xe,
    perm,
    xg,
    wkb,
    wvb,
    padbuf,
    kb,
    vb,
    dkb,
    dvb,
    bias,
    pbuf,
    stats,
    gkb,
    gvb,
    v_slots_x,
    v_sum_x,
    v_slots_near,
    v_sum_near,
    v_slots_stride,
    k_slots_near,
    k_sum_near,
    k_slots_x,
    k_sum_x,
    k_slots_stride,
    send_sem,
    recv_sem,
):
    nx, nz, ny, nc = sizes
    seq_count = nx * nz
    slot_count, tok, enc = nb_ref.shape
    rows_each = wk_ref.shape[0]
    width = wk_ref.shape[1]
    heads = width // HS
    queries = q_ref.shape[0]
    block_len = queries // 2
    padded = seq_count * PAD
    tp_count = ny * nc
    keys = tp_count * slot_count * tok
    scale = HS ** (-0.5)
    seq, tp = lax.axis_index("seq"), lax.axis_index("tp")
    x, z = seq // nz, lax.rem(seq, nz)
    y, core = tp // nc, lax.rem(tp, nc)

    def at_x(i):
        return {"seq": i * nz + z, "tp": tp}

    def at_z(i):
        return {"seq": x * nz + i, "tp": tp}

    def at_y(i):
        return {"seq": seq, "tp": i * nc + core}

    other_core = {"seq": seq, "tp": y * nc + (1 - core)}

    def at_seq(i):
        return {"seq": i, "tp": tp}

    nq, zq, zr = nz // QUAD, z // QUAD, lax.rem(z, QUAD)

    def x_peer(d):
        return at_x(lax.rem(x + d, nx))

    def y_peer(d):
        return at_y(lax.rem(y + d, ny))

    def z_peer(d):
        return at_z(lax.rem(z + d + nz, nz))

    z_near = (1, -1, 2)
    peers = [z_peer(d) for d in (1, -1, 2, -2)]
    peers += [z_peer(QUAD * d) for d in range(1, nq)]
    peers += [x_peer(d) for d in range(1, nx)]
    peers += [y_peer(d) for d in range(1, ny)]
    peers += [other_core]
    for o in range(1, REACH):
        peers.append(at_seq(lax.rem(seq + o, seq_count)))
        peers.append(at_seq(lax.rem(seq + seq_count - o, seq_count)))
    barrier = pltpu.get_barrier_semaphore()
    for peer in peers:
        pl.semaphore_signal(barrier, inc=1, device_id=peer, device_id_type=MESH)

    for source, target in ((wk_ref, wkb), (wv_ref, wvb)):
        padbuf[...] = jnp.zeros_like(padbuf)
        padbuf[0:rows_each, :] = source[...].astype(F32)
        target[zq, zr, x] = padbuf[...].astype(BF16)
    per = slot_count // REACH
    nbf[0:per] = nb_ref[0:per]
    pl.semaphore_wait(barrier, len(peers))

    sems = Sems(send_sem, recv_sem)

    def send(block, devices):
        return [sems.copy(block, block, device) for device in devices]

    stride_devices = [z_peer(QUAD * d) for d in range(1, nq)]
    near_devices = [z_peer(d) for d in z_near]
    x_devices = [x_peer(d) for d in range(1, nx)]
    y_devices = [y_peer(d) for d in range(1, ny)]
    k_stride = send(wkb.at[zq, zr, x], stride_devices)
    v_stride = send(wvb.at[zq, zr, x], stride_devices)
    arriving = {}
    for o in range(1, REACH):
        arriving[o] = sems.copy(
            nb_ref.at[pl.ds(per * o, per)],
            nbf.at[pl.ds(per * o, per)],
            at_seq(lax.rem(seq + seq_count - o, seq_count)),
        )

    first_count = counts_ref[0]
    member = []
    for r in range(slot_count):
        m = jnp.int32(0)
        for i in range(slot_count):
            m = m + jnp.where(owner_ref[i] == r, jnp.where(first_count <= i, 1, 0), 0)
        member.append(m)

    def place():
        col = lax.broadcasted_iota(jnp.int32, (8, padded), 1)
        chunk, e = col // PAD, lax.rem(col, PAD)
        owner = lax.rem(chunk, nx) * nz + chunk // nx
        want = jnp.where(e < rows_each, owner * rows_each + e, -1)[0:1]
        row = lax.broadcasted_iota(jnp.int32, (enc, padded), 0)
        perm[...] = jnp.where(row == want, 1.0, 0.0).astype(BF16)

    def make_bias():
        slot = lax.rem(lax.broadcasted_iota(jnp.int32, (8, keys), 1) // tok, slot_count)
        owned = jnp.zeros((8, keys), jnp.int32)
        for r in range(slot_count):
            owned = jnp.where(slot == r, member[r], owned)
        block = lax.broadcasted_iota(jnp.int32, (queries, keys), 0) // block_len
        bias[...] = jnp.where(block == owned[0:1], 0.0, -jnp.inf)

    def encode(r0, r1):
        n = (r1 - r0) * tok
        states = nbf[r0:r1].reshape(n, enc)
        slot = r0 + lax.broadcasted_iota(jnp.int32, (n, queries), 0) // tok
        owned = jnp.zeros((n, queries), jnp.int32)
        for r in range(r0, r1):
            owned = jnp.where(slot == r, member[r], owned)
        token_block = lax.broadcasted_iota(jnp.int32, (n, queries), 1) // block_len
        ok = token_block == owned
        for h in range(enc // HS):
            cols = slice(h * HS, (h + 1) * HS)
            mine = states[:, cols]
            s = dot(mine, kv_ref[:, cols], ((1,), (1,))) * scale
            s = jnp.where(ok, s, -jnp.inf)
            p = jnp.exp(s - jnp.max(s, axis=1, keepdims=True))
            w = (p / jnp.sum(p, axis=1, keepdims=True)).astype(BF16)
            mixed = dot(w, kv_ref[:, enc + h * HS : enc + (h + 1) * HS])
            xe[r0 * tok : r1 * tok, cols] = (mine.astype(F32) + mixed).astype(BF16)
        spread = dot(xe[r0 * tok : r1 * tok, :], perm[...]).astype(BF16)
        xg[y, core, r0:r1] = spread.reshape(r1 - r0, tok, padded)
        mine = xg.at[y, core, pl.ds(r0, r1 - r0)]
        return send(mine, y_devices)

    def cross(r0, r1):
        block = xg.at[:, core, pl.ds(r0, r1 - r0)]
        return send(block, [other_core])

    place()
    cut0, cut1 = per, 3 * per
    share0 = encode(0, cut0)
    make_bias()
    landed(k_stride)
    k_x = send(wkb.at[:, zr, x], x_devices)
    landed(v_stride)
    v_near = send(wvb.at[:, zr, x], near_devices)
    landed(arriving[o] for o in (1, 2))
    share1 = encode(cut0, cut1)
    landed(k_x)
    k_near = send(wkb.at[:, zr], near_devices)
    landed(v_near)
    v_x = send(wvb.at[:, :, x], x_devices)
    landed(arriving[o] for o in (3, 4))
    share2 = encode(cut1, slot_count)
    landed(share0)
    crossing = cross(0, cut0)
    landed(share1)
    crossing += cross(cut0, cut1)
    landed(share2)
    crossing += cross(cut1, slot_count)
    landed(k_near)
    landed(crossing)

    half_y = ny // 2
    group_rows = keys // 2

    def project(i, weights, target):
        rows = xg[i * half_y : (i + 1) * half_y].reshape(group_rows, padded)
        at = slice(i * group_rows, (i + 1) * group_rows)
        target[at, :] = dot(rows, weights[...].reshape(padded, width)).astype(BF16)

    for i in range(2):
        project(i, wkb, kb)
    landed(v_x)
    for i in range(2):
        project(i, wvb, vb)

    for h in range(heads):
        cols = slice(h * HS, (h + 1) * HS)
        s = dot(q_ref[:, cols], kb[:, cols], ((1,), (1,))) * scale + bias[...]
        p = jnp.exp(s - jnp.max(s, axis=1, keepdims=True))
        inverse = 1.0 / jnp.sum(p, axis=1, keepdims=True)
        out = dot(p.astype(BF16), vb[:, cols]) * inverse
        att_ref[:, cols] = out.astype(BF16)
        grad = g_ref[:, cols]
        delta = jnp.sum(grad.astype(F32) * out, axis=1, keepdims=True)
        stats[h] = jnp.broadcast_to(delta, (queries, HS))
        p = p * inverse
        pbuf[h] = p
        dvb[:, cols] = dot(p.astype(BF16), grad, ((0,), (0,))).astype(BF16)

    row_tile = padded // nq

    def weight_grad(target, source):
        for i in range(nq):
            lhs = xg[:, :, :, :, i * row_tile : (i + 1) * row_tile].reshape(keys, row_tile)
            part = dot(lhs, source[...], ((0,), (0,)))
            target[i] = part.astype(BF16).reshape(QUAD, nx, PAD, width)

    def exchange_x(block, slots):
        return [
            sems.copy(block(lax.rem(x + d, nx)), slots.at[d - 1], x_peer(d)) for d in range(1, nx)
        ]

    def exchange_near(block, slots):
        half = nq // 2
        copies = []
        for d in (1, -1):
            dst = slots.at[0 if d == 1 else 1]
            copies.append(sems.copy(block(lax.rem(zr + d + QUAD, QUAD)), dst, z_peer(d)))
        for d, first in ((2, 0), (-2, half)):
            src = block(lax.rem(zr + 2, QUAD)).at[pl.ds(first, half)]
            copies.append(sems.copy(src, slots.at[2, pl.ds(first, half)], z_peer(d)))
        return copies

    def exchange_stride(block, slots):
        return [
            sems.copy(block(lax.rem(zq + d, nq)), slots.at[d - 1], z_peer(QUAD * d))
            for d in range(1, nq)
        ]

    def total(own, slots):
        result = own.astype(F32)
        for i in range(slots.shape[0]):
            result = result + slots[i].astype(F32)
        return result

    weight_grad(gvb, dvb)
    gv_x = exchange_x(lambda i: gvb.at[:, :, i], v_slots_x)

    for h in range(heads):
        cols = slice(h * HS, (h + 1) * HS)
        dp = dot(g_ref[:, cols], vb[:, cols], ((1,), (1,)))
        ds = (pbuf[h] * (dp - stats[h][:, 0:1])).astype(BF16)
        dq_ref[:, cols] = dot(ds, kb[:, cols]) * scale
        dkb[:, cols] = (dot(ds, q_ref[:, cols], ((0,), (0,))) * scale).astype(BF16)
    weight_grad(gkb, dkb)
    gk_near = exchange_near(lambda i: gkb.at[:, i], k_slots_near)
    landed(gv_x)
    v_sum_x[...] = total(gvb[:, :, x], v_slots_x).astype(BF16)
    gv_near = exchange_near(lambda i: v_sum_x.at[:, i], v_slots_near)
    landed(gk_near)
    k_sum_near[...] = total(gkb[:, zr], k_slots_near).astype(BF16)
    gk_x = exchange_x(lambda i: k_sum_near.at[:, i], k_slots_x)
    landed(gv_near)
    v_sum_near[...] = total(v_sum_x[:, zr], v_slots_near).astype(BF16)
    gv_stride = exchange_stride(lambda i: v_sum_near.at[i], v_slots_stride)
    landed(gk_x)
    k_sum_x[...] = total(k_sum_near[:, x], k_slots_x).astype(BF16)
    gk_stride = exchange_stride(lambda i: k_sum_x.at[i], k_slots_stride)
    landed(gv_stride)
    gv_ref[...] = total(v_sum_near[zq], v_slots_stride)[0:rows_each]
    landed(gk_stride)
    gk_ref[...] = total(k_sum_x[zq], k_slots_stride)[0:rows_each]
    sems.finish()


def per_device(sizes, queries, block_kv, nb_states, key_weight, value_weight, counts, owner, grad):
    nx, nz, ny, nc = sizes
    tokens, width = queries.shape
    slot_count, tok, enc = nb_states.shape
    rows_each = key_weight.shape[0]
    heads = width // HS
    padded = nx * nz * PAD
    tp_count = ny * nc
    keys = tp_count * slot_count * tok
    nq = nz // QUAD
    copies = 4 * (nx - 1) + 4 * (nq - 1) + 6 + 8 + REACH - 1 + 3 * ny
    vmem = pl.BlockSpec(memory_space=pltpu.VMEM)
    smem = pl.BlockSpec(memory_space=pltpu.SMEM)
    scratch = [
        pltpu.VMEM((slot_count, tok, enc), BF16),
        pltpu.VMEM((slot_count * tok, enc), BF16),
        pltpu.VMEM((enc, padded), BF16),
        pltpu.VMEM((ny, nc, slot_count, tok, padded), BF16),
        pltpu.VMEM((nq, QUAD, nx, PAD, width), BF16),
        pltpu.VMEM((nq, QUAD, nx, PAD, width), BF16),
        pltpu.VMEM((PAD, width), F32),
        pltpu.VMEM((keys, width), BF16),
        pltpu.VMEM((keys, width), BF16),
        pltpu.VMEM((keys, width), BF16),
        pltpu.VMEM((keys, width), BF16),
        pltpu.VMEM((tokens, keys), F32),
        pltpu.VMEM((heads, tokens, keys), F32),
        pltpu.VMEM((heads, tokens, HS), F32),
        pltpu.VMEM((nq, QUAD, nx, PAD, width), BF16),
        pltpu.VMEM((nq, QUAD, nx, PAD, width), BF16),
        pltpu.VMEM((nx - 1, nq, QUAD, PAD, width), BF16),
        pltpu.VMEM((nq, QUAD, PAD, width), BF16),
        pltpu.VMEM((3, nq, PAD, width), BF16),
        pltpu.VMEM((nq, PAD, width), BF16),
        pltpu.VMEM((nq - 1, PAD, width), BF16),
        pltpu.VMEM((3, nq, nx, PAD, width), BF16),
        pltpu.VMEM((nq, nx, PAD, width), BF16),
        pltpu.VMEM((nx - 1, nq, PAD, width), BF16),
        pltpu.VMEM((nq, PAD, width), BF16),
        pltpu.VMEM((nq - 1, PAD, width), BF16),
        pltpu.SemaphoreType.DMA((copies,)),
        pltpu.SemaphoreType.DMA((copies,)),
    ]
    return pl.pallas_call(
        functools.partial(kernel, sizes),
        out_shape=(
            jax.ShapeDtypeStruct((tokens, width), BF16),
            jax.ShapeDtypeStruct((tokens, width), F32),
            jax.ShapeDtypeStruct((rows_each, width), F32),
            jax.ShapeDtypeStruct((rows_each, width), F32),
        ),
        in_specs=[vmem, vmem, vmem, vmem, vmem, smem, smem, vmem],
        out_specs=(vmem, vmem, vmem, vmem),
        scratch_shapes=scratch,
        compiler_params=pltpu.CompilerParams(
            collective_id=0, has_side_effects=True, vmem_limit_bytes=56 * 1024 * 1024
        ),
        cost_estimate=pl.CostEstimate(
            flops=8 * 10**9, bytes_accessed=2 * 10**6, transcendentals=10**6
        ),
    )(queries, block_kv, nb_states, key_weight, value_weight, counts, owner, grad)


def solution(mesh, sizes=(4, 16, 4, 2)):
    in_specs = (
        P("seq", "tp"),
        P("seq", None),
        P("seq", "tp", None),
        P("seq", "tp"),
        P("seq", "tp"),
        P("seq"),
        P("seq"),
        P("seq", "tp"),
    )
    out_specs = (P("seq", "tp"), P("seq", "tp"), P("seq", "tp"), P("seq", "tp"))
    return jax.shard_map(
        functools.partial(per_device, sizes),
        mesh=mesh,
        in_specs=in_specs,
        out_specs=out_specs,
        check_vma=False,
    )
```

time: 826 us -> 93.5 us (0.11); the launches traced: 816 us -> 93.2 us
  waiting for transfers between devices: 405 us -> 0 us
  blocking collectives: 165 us -> 0 us
  starting transfers between devices: 152 us -> 0 us
  Pallas kernels: 0 us -> 88.8 us
  local copies, waits for them, and re-layouts: 44.7 us -> 3.76 us
  matrix products: 24.5 us -> 0 us
  between operations: 15.7 us -> 0.65 us
  other arithmetic: 9.05 us -> 0 us
    unnamed x3 -> x0, waiting for transfers between devices: 303 us -> none
    all_gather x2 -> x0, blocking collectives: 165 us -> none  [the longest x1 89.8 us: per_device(): lax.all_gather(key_weight, 'seq', axis=0, tiled=True)]
    ppermute x32 -> x0, starting transfers between devices: 152 us -> none  [shifted(): return lax.ppermute(block, axis, route)]
    ppermute x32 -> x0, waiting for transfers between devices: 102 us -> none  [shifted(): return lax.ppermute(block, axis, route)]
    pallas_call x0 -> x1, Pallas kernels: none -> 88.8 us  [per_device(): pl.pallas_call(functools.partial(kernel, sizes), out_shape=(jax.ShapeDtyp...]
    dot_general x13 -> x0, matrix products: 24.5 us -> none  [the longest x1 4.47 us: per_device(): lax.dot_general(encoded_flat, grads_flat, (((0,), (0,)), ((), ())), prefe...]
    concatenate x12 -> x0, local copies, waits for them, and re-layouts: 12.3 us -> none  [the longest x1 11.8 us: per_device(): slot_kv = jnp.concatenate(got_kv, axis=0)]
  transfers between devices with their start and end apart: 34 -> 0, of which waited for: 11 -> 0; matrix products, arithmetic and copies ran while one was open for 2% -> 0% of each run, Pallas kernels for 0% -> 0%
where the time goes in v1:
time: 93.5 us; the launch traced here: 93.2 us
  Pallas kernels  88.8 us (95%)
  local copies, waits for them, and re-layouts  3.76 us (4%)
    pallas_call x1, Pallas kernels, per_device(): pl.pallas_call(functools.partial(kernel, sizes), out_shape=(jax.ShapeDtyp...  88.8 us
    unnamed x10, local copies, waits for them, and re-layouts  3.76 us

profile of v1, /device:TPU:1, one launch (start us, length us, event | category | flops | bytes accessed | tf_op | source)
XLA Modules:
  0.0 93.2 jit_solution(13040461142806550454)
XLA Ops:
  0.6 88.8 %shard_map.111 = (bf16[128,512]{1,0:T(8,128)(2,1)}, f32[128,512]{1,0:T(8,128)}, f32[14,512]{1,0:T(8,128)}, f32[14,512]{1,0:T(8,128)}) custom-call(bf16[128,512]{1,0:T(8,128)(2,1)} %q_ref.1, bf16[128,1792]{1,0:T(8,128)(2,1)} %kv_ref.1, bf16[10,16,896]{2,1,0:T(8,128)(2,1)} %nb_ref.1, bf16[14,512]{1,0:T(8,128)(2,1)} %wk_ref.1, bf16[14,512]{1,0:T(8,128)(2,1)} %wv_ref.1, ...), custom_call_target="tpu_custom_call" | custom-call | flops 8000000000 | bytes 2000000 | tf_op jit(solution)/shard_map/pallas_call | solution.py:391
  89.5 0.0 copy-start
  89.5 1.6 %copy.16 = bf16[128,512]{1,0:T(8,128)(2,1)} copy(bf16[128,512]{1,0:T(8,128)(2,1)} %get-tuple-element.8) | data formatting | bytes 262144
  91.1 0.0 copy-done
  91.1 0.0 copy-start.2
  91.1 0.7 copy.17
  91.8 0.1 copy-done.2
  91.8 0.0 copy-start.1
  91.8 0.6 copy.18
  92.5 0.2 copy-done.1
  92.6 0.6 copy.19
Async XLA Ops:
  89.5 1.6 %copy-start = (f32[128,512]{1,0:T(8,128)S(1)}, f32[128,512]{1,0:T(8,128)}, u32[]{:S(2)}) copy-start(f32[128,512]{1,0:T(8,128)} %get-tuple-element.9) | copy-start | bytes 786436
  91.1 0.8 copy-start.2
  91.8 0.8 copy-start.1

commit v2 on v1

--- a/solution.py
+++ b/solution.py
@@ -208,15 +208,19 @@
             owned = jnp.where(slot == r, member[r], owned)
         token_block = lax.broadcasted_iota(jnp.int32, (n, queries), 1) // block_len
         ok = token_block == owned
-        for h in range(enc // HS):
-            cols = slice(h * HS, (h + 1) * HS)
-            mine = states[:, cols]
-            s = dot(mine, kv_ref[:, cols], ((1,), (1,))) * scale
-            s = jnp.where(ok, s, -jnp.inf)
-            p = jnp.exp(s - jnp.max(s, axis=1, keepdims=True))
-            w = (p / jnp.sum(p, axis=1, keepdims=True)).astype(BF16)
-            mixed = dot(w, kv_ref[:, enc + h * HS : enc + (h + 1) * HS])
-            xe[r0 * tok : r1 * tok, cols] = (mine.astype(F32) + mixed).astype(BF16)
+        rows = slice(r0 * tok, r1 * tok)
+        parts = [slice(h * HS, (h + 1) * HS) for h in range(enc // HS)]
+        scores = [dot(states[:, c], kv_ref[:, c], ((1,), (1,))) for c in parts]
+        scores = [jnp.where(ok, s * scale, -jnp.inf) for s in scores]
+        tops = [jnp.max(s, axis=1, keepdims=True) for s in scores]
+        scores = [jnp.exp(s - t) for s, t in zip(scores, tops)]
+        sums = [jnp.sum(p, axis=1, keepdims=True) for p in scores]
+        scores = [(p / t).astype(BF16) for p, t in zip(scores, sums)]
+        mixed = [
+            dot(w, kv_ref[:, enc + h * HS : enc + (h + 1) * HS]) for h, w in enumerate(scores)
+        ]
+        for c, m in zip(parts, mixed):
+            xe[rows, c] = (states[:, c].astype(F32) + m).astype(BF16)
         spread = dot(xe[r0 * tok : r1 * tok, :], perm[...]).astype(BF16)
         xg[y, core, r0:r1] = spread.reshape(r1 - r0, tok, padded)
         mine = xg.at[y, core, pl.ds(r0, r1 - r0)]
@@ -231,15 +235,25 @@
     share0 = encode(0, cut0)
     make_bias()
     landed(k_stride)
-    k_x = send(wkb.at[:, zr, x], x_devices)
+    low, high = pl.ds(0, width // 2), pl.ds(width // 2, width // 2)
+    k_near = send(wkb.at[:, zr, x, :, low], near_devices)
+    l_x = send(wkb.at[:, zr, x, :, high], x_devices)
+    k_x = send(wkb.at[:, zr, x, :, low], x_devices)
+    l_near = send(wkb.at[:, zr, x, :, high], near_devices)
     landed(v_stride)
     v_near = send(wvb.at[:, zr, x], near_devices)
+    v_x = send(wvb.at[:, zr, x], x_devices)
     landed(arriving[o] for o in (1, 2))
     share1 = encode(cut0, cut1)
-    landed(k_x)
-    k_near = send(wkb.at[:, zr], near_devices)
-    landed(v_near)
-    v_x = send(wvb.at[:, :, x], x_devices)
+    for i, d in enumerate(z_near):
+        landed(k_near[i : i + 1])
+        k_x += send(wkb.at[:, lax.rem(zr + QUAD - d, QUAD), x, :, low], x_devices)
+    for d in range(1, nx):
+        landed(l_x[d - 1 : d])
+        l_near += send(wkb.at[:, zr, lax.rem(x + nx - d, nx), :, high], near_devices)
+    for i, d in enumerate(z_near):
+        landed(v_near[i : i + 1])
+        v_x += send(wvb.at[:, lax.rem(zr + QUAD - d, QUAD), x], x_devices)
     landed(arriving[o] for o in (3, 4))
     share2 = encode(cut1, slot_count)
     landed(share0)
@@ -248,7 +262,8 @@
     crossing += cross(cut0, cut1)
     landed(share2)
     crossing += cross(cut1, slot_count)
-    landed(k_near)
+    landed(k_x)
+    landed(l_near)
     landed(crossing)
 
     half_y = ny // 2
@@ -265,19 +280,21 @@
     for i in range(2):
         project(i, wvb, vb)
 
-    for h in range(heads):
-        cols = slice(h * HS, (h + 1) * HS)
-        s = dot(q_ref[:, cols], kb[:, cols], ((1,), (1,))) * scale + bias[...]
-        p = jnp.exp(s - jnp.max(s, axis=1, keepdims=True))
-        inverse = 1.0 / jnp.sum(p, axis=1, keepdims=True)
-        out = dot(p.astype(BF16), vb[:, cols]) * inverse
-        att_ref[:, cols] = out.astype(BF16)
-        grad = g_ref[:, cols]
-        delta = jnp.sum(grad.astype(F32) * out, axis=1, keepdims=True)
+    parts = [slice(h * HS, (h + 1) * HS) for h in range(heads)]
+    scores = [dot(q_ref[:, c], kb[:, c], ((1,), (1,))) for c in parts]
+    scores = [s * scale + bias[...] for s in scores]
+    tops = [jnp.max(s, axis=1, keepdims=True) for s in scores]
+    weights = [jnp.exp(s - t) for s, t in zip(scores, tops)]
+    inverse = [1.0 / jnp.sum(p, axis=1, keepdims=True) for p in weights]
+    outs = [dot(p.astype(BF16), vb[:, c]) * t for p, c, t in zip(weights, parts, inverse)]
+    weights = [p * t for p, t in zip(weights, inverse)]
+    for h, c in enumerate(parts):
+        pbuf[h] = weights[h]
+        dvb[:, c] = dot(weights[h].astype(BF16), g_ref[:, c], ((0,), (0,))).astype(BF16)
+    for h, c in enumerate(parts):
+        att_ref[:, c] = outs[h].astype(BF16)
+        delta = jnp.sum(g_ref[:, c].astype(F32) * outs[h], axis=1, keepdims=True)
         stats[h] = jnp.broadcast_to(delta, (queries, HS))
-        p = p * inverse
-        pbuf[h] = p
-        dvb[:, cols] = dot(p.astype(BF16), grad, ((0,), (0,))).astype(BF16)
 
     row_tile = padded // nq
 
@@ -318,20 +335,29 @@
     weight_grad(gvb, dvb)
     gv_x = exchange_x(lambda i: gvb.at[:, :, i], v_slots_x)
 
-    for h in range(heads):
-        cols = slice(h * HS, (h + 1) * HS)
-        dp = dot(g_ref[:, cols], vb[:, cols], ((1,), (1,)))
-        ds = (pbuf[h] * (dp - stats[h][:, 0:1])).astype(BF16)
-        dq_ref[:, cols] = dot(ds, kb[:, cols]) * scale
-        dkb[:, cols] = (dot(ds, q_ref[:, cols], ((0,), (0,))) * scale).astype(BF16)
+    dps = [dot(g_ref[:, c], vb[:, c], ((1,), (1,))) for c in parts]
+    dss = [(pbuf[h] * (dp - stats[h][:, 0:1])).astype(BF16) for h, dp in enumerate(dps)]
+    for ds, c in zip(dss, parts):
+        dkb[:, c] = (dot(ds, q_ref[:, c], ((0,), (0,))) * scale).astype(BF16)
     weight_grad(gkb, dkb)
-    gk_near = exchange_near(lambda i: gkb.at[:, i], k_slots_near)
+    gk_near = []
+    for d in range(1, nx + 1):
+        to = lax.rem(x + d, nx)
+        gk_near.append(
+            exchange_near(lambda i, to=to: gkb.at[:, i, to], k_slots_near.at[:, :, to])
+        )
+    for ds, c in zip(dss, parts):
+        dq_ref[:, c] = dot(ds, kb[:, c]) * scale
     landed(gv_x)
     v_sum_x[...] = total(gvb[:, :, x], v_slots_x).astype(BF16)
     gv_near = exchange_near(lambda i: v_sum_x.at[:, i], v_slots_near)
-    landed(gk_near)
-    k_sum_near[...] = total(gkb[:, zr], k_slots_near).astype(BF16)
-    gk_x = exchange_x(lambda i: k_sum_near.at[:, i], k_slots_x)
+    gk_x = []
+    for d in range(1, nx + 1):
+        to = lax.rem(x + d, nx)
+        landed(gk_near[d - 1])
+        k_sum_near[:, to] = total(gkb[:, zr, to], k_slots_near.at[:, :, to]).astype(BF16)
+        if d < nx:
+            gk_x.append(sems.copy(k_sum_near.at[:, to], k_slots_x.at[d - 1], x_peer(d)))
     landed(gv_near)
     v_sum_near[...] = total(v_sum_x[:, zr], v_slots_near).astype(BF16)
     gv_stride = exchange_stride(lambda i: v_sum_near.at[i], v_slots_stride)
@@ -355,7 +381,8 @@
     tp_count = ny * nc
     keys = tp_count * slot_count * tok
     nq = nz // QUAD
-    copies = 4 * (nx - 1) + 4 * (nq - 1) + 6 + 8 + REACH - 1 + 3 * ny
+    copies = 4 * (nq - 1) + 4 * (nx - 1) + 2 * 3 * nx + (nx - 1) * 3 + 4 * nx + 4
+    copies += REACH - 1 + 3 * ny + 4 * (nx - 1) + 3 * nx
     vmem = pl.BlockSpec(memory_space=pltpu.VMEM)
     smem = pl.BlockSpec(memory_space=pltpu.SMEM)
     scratch = [

time: 93.5 us -> 92.1 us (0.985)
  Pallas kernels: 88.8 us -> 87.4 us
    pallas_call x1, Pallas kernels: 88.8 us -> 87.4 us  [per_device(): pl.pallas_call(functools.partial(kernel, sizes), out_shape=(jax.ShapeDtyp...]
where the time goes in v2:
time: 92.1 us; the launch traced here: 91.8 us
  Pallas kernels  87.4 us (95%)
  local copies, waits for them, and re-layouts  3.76 us (4%)
    pallas_call x1, Pallas kernels, per_device(): pl.pallas_call(functools.partial(kernel, sizes), out_shape=(jax.ShapeDtyp...  87.4 us
    unnamed x10, local copies, waits for them, and re-layouts  3.76 us

profile of v2, /device:TPU:1, one launch (start us, length us, event | category | flops | bytes accessed | tf_op | source)
XLA Modules:
  0.0 91.8 jit_solution(12278649567406514512)
XLA Ops:
  0.6 87.4 %shard_map.111 = (bf16[128,512]{1,0:T(8,128)(2,1)}, f32[128,512]{1,0:T(8,128)}, f32[14,512]{1,0:T(8,128)}, f32[14,512]{1,0:T(8,128)}) custom-call(bf16[128,512]{1,0:T(8,128)(2,1)} %q_ref.1, bf16[128,1792]{1,0:T(8,128)(2,1)} %kv_ref.1, bf16[10,16,896]{2,1,0:T(8,128)(2,1)} %nb_ref.1, bf16[14,512]{1,0:T(8,128)(2,1)} %wk_ref.1, bf16[14,512]{1,0:T(8,128)(2,1)} %wv_ref.1, ...), custom_call_target="tpu_custom_call" | custom-call | flops 8000000000 | bytes 2000000 | tf_op jit(solution)/shard_map/pallas_call | solution.py:418
  88.1 0.0 copy-start
  88.1 1.6 %copy.16 = bf16[128,512]{1,0:T(8,128)(2,1)} copy(bf16[128,512]{1,0:T(8,128)(2,1)} %get-tuple-element.8) | data formatting | bytes 262144
  89.7 0.0 copy-done
  89.7 0.0 copy-start.2
  89.7 0.7 copy.17
  90.4 0.1 copy-done.2
  90.4 0.0 copy-start.1
  90.5 0.6 copy.18
  91.1 0.2 copy-done.1
  91.2 0.6 copy.19
Async XLA Ops:
  88.1 1.6 %copy-start = (f32[128,512]{1,0:T(8,128)S(1)}, f32[128,512]{1,0:T(8,128)}, u32[]{:S(2)}) copy-start(f32[128,512]{1,0:T(8,128)} %get-tuple-element.9) | copy-start | bytes 786436
  89.7 0.8 copy-start.2
  90.4 0.8 copy-start.1

commit v3 on v2

--- a/solution.py
+++ b/solution.py
@@ -244,24 +244,24 @@
     v_near = send(wvb.at[:, zr, x], near_devices)
     v_x = send(wvb.at[:, zr, x], x_devices)
     landed(arriving[o] for o in (1, 2))
-    share1 = encode(cut0, cut1)
+    share1 = encode(1 * per, 3 * per)
     for i, d in enumerate(z_near):
         landed(k_near[i : i + 1])
         k_x += send(wkb.at[:, lax.rem(zr + QUAD - d, QUAD), x, :, low], x_devices)
+    landed(arriving[o] for o in (3, 4))
+    share2 = encode(3 * per, 5 * per)
+    for i, d in enumerate(z_near):
+        landed(v_near[i : i + 1])
+        v_x += send(wvb.at[:, lax.rem(zr + QUAD - d, QUAD), x], x_devices)
+    landed(share0)
+    crossing = cross(0, per)
+    landed(share1)
+    crossing += cross(1 * per, 3 * per)
     for d in range(1, nx):
         landed(l_x[d - 1 : d])
         l_near += send(wkb.at[:, zr, lax.rem(x + nx - d, nx), :, high], near_devices)
-    for i, d in enumerate(z_near):
-        landed(v_near[i : i + 1])
-        v_x += send(wvb.at[:, lax.rem(zr + QUAD - d, QUAD), x], x_devices)
-    landed(arriving[o] for o in (3, 4))
-    share2 = encode(cut1, slot_count)
-    landed(share0)
-    crossing = cross(0, cut0)
-    landed(share1)
-    crossing += cross(cut0, cut1)
     landed(share2)
-    crossing += cross(cut1, slot_count)
+    crossing += cross(3 * per, 5 * per)
     landed(k_x)
     landed(l_near)
     landed(crossing)
@@ -382,7 +382,7 @@
     keys = tp_count * slot_count * tok
     nq = nz // QUAD
     copies = 4 * (nq - 1) + 4 * (nx - 1) + 2 * 3 * nx + (nx - 1) * 3 + 4 * nx + 4
-    copies += REACH - 1 + 3 * ny + 4 * (nx - 1) + 3 * nx
+    copies += REACH - 1 + 5 * ny + 4 * (nx - 1) + 3 * nx
     vmem = pl.BlockSpec(memory_space=pltpu.VMEM)
     smem = pl.BlockSpec(memory_space=pltpu.SMEM)
     scratch = [

time: 92.1 us -> 89.5 us (0.972)
  the two profiles are of different devices: /device:TPU:1 before, /device:TPU:22 now
where the time goes in v3:
time: 89.5 us; the launch traced here: 89.2 us
  Pallas kernels  84.8 us (95%)
  local copies, waits for them, and re-layouts  3.76 us (4%)
    pallas_call x1, Pallas kernels, per_device(): pl.pallas_call(functools.partial(kernel, sizes), out_shape=(jax.ShapeDtyp...  84.8 us
    unnamed x10, local copies, waits for them, and re-layouts  3.76 us

profile of v3, /device:TPU:22, one launch (start us, length us, event | category | flops | bytes accessed | tf_op | source)
XLA Modules:
  0.0 89.2 jit_solution(17200123408260080451)
XLA Ops:
  0.6 84.8 %shard_map.111 = (bf16[128,512]{1,0:T(8,128)(2,1)}, f32[128,512]{1,0:T(8,128)}, f32[14,512]{1,0:T(8,128)}, f32[14,512]{1,0:T(8,128)}) custom-call(bf16[128,512]{1,0:T(8,128)(2,1)} %q_ref.1, bf16[128,1792]{1,0:T(8,128)(2,1)} %kv_ref.1, bf16[10,16,896]{2,1,0:T(8,128)(2,1)} %nb_ref.1, bf16[14,512]{1,0:T(8,128)(2,1)} %wk_ref.1, bf16[14,512]{1,0:T(8,128)(2,1)} %wv_ref.1, ...), custom_call_target="tpu_custom_call" | custom-call | flops 8000000000 | bytes 2000000 | tf_op jit(solution)/shard_map/pallas_call | solution.py:418
  85.4 0.0 copy-start
  85.4 1.6 %copy.16 = bf16[128,512]{1,0:T(8,128)(2,1)} copy(bf16[128,512]{1,0:T(8,128)(2,1)} %get-tuple-element.8) | data formatting | bytes 262144
  87.1 0.0 copy-done
  87.1 0.0 copy-start.2
  87.1 0.7 copy.17
  87.8 0.1 copy-done.2
  87.8 0.0 copy-start.1
  87.8 0.6 copy.18
  88.4 0.2 copy-done.1
  88.6 0.6 copy.19
Async XLA Ops:
  85.4 1.6 %copy-start = (f32[128,512]{1,0:T(8,128)S(1)}, f32[128,512]{1,0:T(8,128)}, u32[]{:S(2)}) copy-start(f32[128,512]{1,0:T(8,128)} %get-tuple-element.9) | copy-start | bytes 786436
  87.1 0.8 copy-start.2
  87.8 0.8 copy-start.1
